TPU v7x, 256 devices: a whole 4x4x8 slice. The times are simulated.
256 devices in a mesh: leaf: 8 (over y, core), front: 32 (over z, x).
Axes of the slice: x: 4, y: 4, z: 8, core: 2. Of those that a mesh axis runs over, the one named last changes fastest.
Arguments:
- leaf_inverse: bfloat16 [8192, 128, 128], P(('leaf', 'front')), may hold values from -0.5 to 0.5
- leaf_rhs: bfloat16 [8192, 128, 256], P(('leaf', 'front')), may hold values from -6 to 6
- off_blocks: bfloat16 [8192, 5, 128, 128], P(('leaf', 'front')), may hold values from -0.0546875 to 0.0546875
- block_rows: int32 [8192, 5], P(('leaf', 'front')), may hold values from 0 to 63
- fill_count: int32 [8192], P(('leaf', 'front')), may hold values from 1 to 5
- sep_rhs: bfloat16 [256, 128, 256], P(('leaf', 'front')), may hold values from -6 to 6
- panel_order: int32 [8, 32], P('leaf'), may hold values from 0 to 31, each once within a row
- sep_inverse: bfloat16 [256, 128, 4096], P(('leaf', 'front')), may hold values from -0.09375 to 0.09375
Outputs:
- leaf_solution: bfloat16 [8192, 128, 256], P(('leaf', 'front'))
- sep_forward: bfloat16 [256, 128, 256], P(('leaf', 'front'))
- sep_solution: float32 [256, 128, 256], P(('leaf', 'front'))
Inputs may be any that keep to these rules, and one draw needn't show every extreme that they name: Each row of panel_order is a permutation of the 32 separators of that front.
All inputs are finite; a program needn't handle non-finite values.
Results may differ from a plain program's by a relative error of at most 0.025.
Values may be sent and summed in bfloat16 or wider, within the bound.
No kernel may reach another device: no remote copies, remote signals or barrier semaphores. Data moves between devices by JAX's collectives and lax.ppermute only.
A program may use at most 128 MiB of HBM per device.

v0:
```python
import jax
import jax.numpy as jnp
from jax import lax
from jax.sharding import PartitionSpec as P


def swapped(shard, axis, bit):
    return lax.ppermute(shard, axis, [(i, i ^ 1 << bit) for i in range(lax.axis_size(axis))])


def on_device(
    leaf_inverse, leaf_rhs, off_blocks, block_rows, fill_count, sep_rhs, panel_order, sep_inverse
):
    block_width = leaf_inverse.shape[1]
    probe_count = leaf_rhs.shape[2]
    owned_count = sep_rhs.shape[0]
    fronts = lax.axis_size("front")
    front_seps = owned_count * fronts
    parity = lax.axis_index("leaf") % 2
    forward = jnp.einsum(
        "kab,kbr->kar", leaf_inverse, leaf_rhs, preferred_element_type=jnp.float32
    ).astype(jnp.bfloat16)
    used_slots = jnp.arange(off_blocks.shape[1], dtype=jnp.int32)[None, :] < fill_count[:, None]
    product = jnp.einsum("kpab,kbr->kpar", off_blocks, forward, preferred_element_type=jnp.float32)
    product = jnp.where(used_slots[:, :, None, None], product, jnp.zeros((), jnp.float32))
    product = product.reshape(-1, block_width, probe_count)
    half_index = block_rows // front_seps
    local_index = block_rows % front_seps
    sibling_flag = (half_index != parity).astype(jnp.int32)
    target = (
        local_index // owned_count * (2 * owned_count)
        + sibling_flag * owned_count
        + local_index % owned_count
    )
    partial_terms = (
        jnp.zeros((2 * front_seps, block_width, probe_count), jnp.float32)
        .at[target.reshape(-1)]
        .add(product)
    )
    shares = lax.psum_scatter(
        partial_terms.astype(jnp.bfloat16), "front", scatter_dimension=0, tiled=True
    ).astype(jnp.float32)
    received = swapped(shares[owned_count:].astype(jnp.bfloat16), "leaf", 0).astype(jnp.float32)
    summed = shares[:owned_count] + received
    separator_in = (sep_rhs.astype(jnp.float32) - summed).astype(jnp.bfloat16)
    arrived = lax.all_gather(separator_in, "front", axis=0, tiled=True)
    arrived_rows = arrived.shape[0]
    columns = sep_inverse
    flat = arrived.reshape(arrived_rows * block_width, probe_count)
    forward_sep = jnp.einsum(
        "sac,cr->sar", columns, flat, preferred_element_type=jnp.float32
    ).astype(jnp.bfloat16)
    owned_rows = lax.dynamic_slice_in_dim(
        panel_order[0], lax.axis_index("front") * owned_count, owned_count
    )
    placed = (
        jnp.zeros((front_seps, block_width, probe_count), jnp.float32)
        .at[owned_rows]
        .set(forward_sep.astype(jnp.float32))
    )
    sep_forward = lax.psum_scatter(
        placed.astype(jnp.bfloat16), "front", scatter_dimension=0, tiled=True
    )
    columns = sep_inverse
    result = jnp.einsum("sac,sar->cr", columns, forward_sep, preferred_element_type=jnp.float32)
    sep_solution = lax.psum_scatter(
        result.reshape(owned_count * lax.axis_size("front"), block_width, probe_count).astype(
            jnp.bfloat16
        ),
        "front",
        scatter_dimension=0,
        tiled=True,
    ).astype(jnp.float32)
    solved = sep_solution.astype(jnp.bfloat16)
    whole_front = lax.all_gather(solved, "front", axis=0, tiled=True)
    other_front = swapped(whole_front, "leaf", 0)
    lower_front = jnp.where(parity == 0, whole_front, other_front)
    upper_front = jnp.where(parity == 0, other_front, whole_front)
    pair_field = jnp.concatenate([lower_front, upper_front], axis=0)
    picked = pair_field[block_rows]
    picked = jnp.where(used_slots[:, :, None, None], picked, jnp.zeros((), jnp.bfloat16))
    pulled = jnp.einsum("kpab,kpar->kbr", off_blocks, picked, preferred_element_type=jnp.float32)
    backward = (forward.astype(jnp.float32) - pulled).astype(jnp.bfloat16)
    leaf_solution = jnp.einsum(
        "kba,kbr->kar", leaf_inverse, backward, preferred_element_type=jnp.float32
    ).astype(jnp.bfloat16)
    return (leaf_solution, sep_forward, sep_solution)


def solution(mesh):
    placed = (
        P(("leaf", "front"), None, None),
        P(("leaf", "front"), None, None),
        P(("leaf", "front"), None, None, None),
        P(("leaf", "front"), None),
        P(("leaf", "front")),
        P(("leaf", "front"), None, None),
        P("leaf", None),
        P(("leaf", "front"), None, None),
    )
    return jax.shard_map(
        on_device,
        mesh=mesh,
        in_specs=placed,
        out_specs=(
            P(("leaf", "front"), None, None),
            P(("leaf", "front"), None, None),
            P(("leaf", "front"), None, None),
        ),
        check_vma=False,
    )
```

profile of v0, /device:TPU:8, one launch (start us, length us, event | category | flops | bytes accessed | tf_op | source)
XLA Modules:
  0.0 925.7 jit_solution(462579910879347742)
XLA Ops:
  7.2 0.0 reduce-scatter.4.cloned.1.call-start
  7.2 0.8 add_select_fusion
  8.1 0.1 copy.27
  8.2 0.1 reshape.113
  8.3 0.9 iota_compare_fusion
  9.2 2.1 convolution_convert_fusion
  11.3 9.0 broadcast_select_fusion
  20.3 21.2 %copy.29 = f32[160,128,256]{2,1,0:T(8,128)} copy(f32[160,128,256]{1,2,0:T(8,128)} %bitcast.45) | data formatting | bytes 41943040 | tf_op jit(solution)/shard_map/reshape | solution.py:26
  41.5 4.3 broadcast_in_dim.40
  45.8 48.0 %scatter_fusion = f32[64,128,256]{2,1,0:T(8,128)} fusion(f32[64,128,256]{2,1,0:T(8,128)} %broadcast_in_dim.40, s32[160]{0:T(256)S(1)} %bitcast.50, f32[160,128,256]{2,1,0:T(8,128)} %copy.29), kind=kCustom, calls=%fused_computation.1 | custom fusion | flops 5242880 | bytes 62915200 | tf_op jit(solution)/shard_map/scatter-add | solution.py:38
  93.8 6.0 convert_element_type.59
  99.7 0.0 reduce-scatter.4.cloned.1.call-update
  99.7 0.0 all-gather.3.cloned.1.call-start
  99.8 224.4 %reduce-scatter.4.cloned.1.call-done = bf16[2,128,256]{2,1,0:T(8,128)(2,1)} async-done(((bf16[64,128,256]{2,1,0:T(8,128)(2,1)}), bf16[2,128,256]{2,1,0:T(8,128)(2,1)}) %reduce-scatter.4.cloned.1.call-update) | async-done | bytes 131088 | tf_op jit(solution)/shard_map/reduce_scatter | solution.py:40
  324.2 0.8 slice.35
  325.0 1.3 collective-permute-done
  326.3 1.5 subtract_convert_fusion
  327.8 0.0 all-gather.3.cloned.1.call-update
  327.8 0.0 reduce-scatter.6.cloned.1.call-start
  327.8 0.7 copy.44
  328.5 75.5 %all-gather.3.cloned.1.call-done = bf16[32,128,256]{2,1,0:T(8,128)(2,1)} async-done(((bf16[1,128,256]{2,1,0:T(8,128)(2,1)}), bf16[32,128,256]{2,1,0:T(8,128)(2,1)}) %all-gather.3.cloned.1.call-update) | async-done | bytes 2097168 | tf_op jit(solution)/shard_map/all_gather | solution.py:46
  404.0 2.4 convolution_convert_fusion.1
  406.4 2.0 convert_bitcast_fusion.1
  408.4 0.0 reduce-scatter.6.cloned.1.call-update
  408.5 0.0 all-gather.5.cloned.1.call-start
  408.5 213.6 %reduce-scatter.6.cloned.1.call-done = bf16[1,128,256]{1,2,0:T(8,128)(2,1)} async-done(((bf16[32,128,256]{1,2,0:T(8,128)(2,1)}), bf16[1,128,256]{1,2,0:T(8,128)(2,1)}) %reduce-scatter.6.cloned.1.call-update) | async-done | bytes 65552 | tf_op jit(solution)/shard_map/reduce_scatter | solution.py:66
  622.1 1.6 copy.31
  623.7 0.0 all-gather.5.cloned.1.call-update
  623.8 0.0 reduce-scatter.8.cloned.1.call-start
  623.8 0.6 constant_dynamic-slice_fusion
  626.4 0.7 and_reduce_fusion
  627.1 0.6 select_bitcast_fusion
  627.6 0.1 copy.36
  627.8 0.2 broadcast_in_dim.45
  628.0 1.3 copy-done.2
  629.4 0.0 reduce-scatter.8.cloned.1.call-update
  629.4 72.0 %all-gather.5.cloned.1.call-done = bf16[32,128,256]{2,1,0:T(8,128)(2,1)} async-done(((bf16[1,128,256]{2,1,0:T(8,128)(2,1)}), bf16[32,128,256]{2,1,0:T(8,128)(2,1)}) %all-gather.5.cloned.1.call-update) | async-done | bytes 2097168 | tf_op jit(solution)/shard_map/all_gather | solution.py:75
  701.3 0.1 copy.32
  701.4 0.1 reshape.121
  701.6 0.8 copy.38
  702.3 3.5 collective-permute-done.1
  705.8 2.5 broadcast_select_fusion.2
  708.3 2.4 pad_maximum_fusion
  710.8 9.8 %gather_fusion = bf16[160,128,256]{2,1,0:T(8,128)(2,1)} fusion(bf16[64,128,256]{2,1,0:T(8,128)(2,1)} %pad_maximum_fusion, s32[1024]{0:T(1024)S(1)} %pad_clamp_fusion), kind=kCustom, calls=%fused_computation | custom fusion | bytes 20972160 | tf_op jit(solution)/shard_map/gather | solution.py:80
  720.6 15.1 %copy.33 = bf16[32,5,128,256]{2,3,1,0:T(8,128)(2,1)} copy(bf16[32,5,128,256]{3,2,1,0:T(8,128)(2,1)} %bitcast.46) | data formatting | bytes 20971520 | tf_op jit(solution)/shard_map/gather | solution.py:80
  735.7 9.2 convert_bitcast_fusion
  744.9 4.1 copy.37
  749.0 170.2 %reduce-scatter.8.cloned.1.call-done = bf16[1,128,256]{2,1,0:T(8,128)(2,1)} async-done(((bf16[32,128,256]{2,1,0:T(8,128)(2,1)}), bf16[1,128,256]{2,1,0:T(8,128)(2,1)}) %reduce-scatter.8.cloned.1.call-update) | async-done | bytes 65552 | tf_op jit(solution)/shard_map/reduce_scatter | solution.py:61
  (26 shorter events, 0.1 us)
Async XLA Ops:
  7.2 2.0 copy-start
  7.2 317.0 %reduce-scatter.4.cloned.1.call-start = ((), (), s32[]{:S(2)}) async-start(), calls=%async_computation.3 | async-start | bytes 4325376 | tf_op jit(solution)/shard_map/reduce_scatter | solution.py:40
  8.3 3.0 copy-start.4
  11.3 9.0 copy-start.3
  99.7 226.6 %copy-start.8 = (bf16[1,128,256]{2,1,0:T(8,128)(2,1)S(1)}, bf16[1,128,256]{2,1,0:T(8,128)(2,1)}, u32[]{:S(2)}) copy-start(bf16[1,128,256]{2,1,0:T(8,128)(2,1)} %param.15) | copy-start | bytes 196612
  99.7 228.1 %copy-start.5 = (bf16[1,128,4096]{2,1,0:T(8,128)(2,1)S(1)}, bf16[1,128,4096]{2,1,0:T(8,128)(2,1)}, u32[]{:S(2)}) copy-start(bf16[1,128,4096]{2,1,0:T(8,128)(2,1)} %param.17) | copy-start | bytes 3145732
  99.7 304.3 %all-gather.3.cloned.1.call-start = ((), (), s32[]{:S(2)}) async-start(), calls=%async_computation.4 | async-start | bytes 2162688 | tf_op jit(solution)/shard_map/all_gather | solution.py:46
  325.0 1.3 collective-permute-start
  327.8 294.3 %reduce-scatter.6.cloned.1.call-start = ((), (), s32[]{:S(2)}) async-start(), calls=%async_computation.5 | async-start | bytes 2162688 | tf_op jit(solution)/shard_map/reduce_scatter | solution.py:66
  404.0 219.8 %copy-start.10 = (s32[1,32]{1,0:T(1,128)S(1)}, s32[1,32]{1,0:T(1,128)}, u32[]{:S(2)}) copy-start(s32[1,32]{1,0:T(1,128)} %param.16) | copy-start | bytes 388
  404.0 222.3 %copy-start.9 = (s32[3]{0:T(128)S(1)}, s32[3]{0:T(128)}, u32[]{:S(2)}) copy-start(s32[3]{0:T(128)} %constant.102.clone.1) | copy-start | bytes 40
  408.5 292.9 %all-gather.5.cloned.1.call-start = ((), (), s32[]{:S(2)}) async-start(), calls=%async_computation.6 | async-start | bytes 2162688 | tf_op jit(solution)/shard_map/all_gather | solution.py:75
  622.1 79.5 %copy-start.7 = (bf16[1,128,256]{1,2,0:T(8,128)(2,1)S(1)}, bf16[1,128,256]{1,2,0:T(8,128)(2,1)}, u32[]{:S(2)}) copy-start(bf16[1,128,256]{1,2,0:T(8,128)(2,1)} %reduce-scatter.6.cloned.1.call-done) | copy-start | bytes 196612
  623.8 295.4 %reduce-scatter.8.cloned.1.call-start = ((), (), s32[]{:S(2)}) async-start(), calls=%async_computation.7 | async-start | bytes 2162688 | tf_op jit(solution)/shard_map/reduce_scatter | solution.py:61
  628.0 1.3 copy-start.2
  701.3 4.5 collective-permute-start.1
  720.6 15.1 %copy-start.6 = (bf16[32,128,128]{2,1,0:T(8,128)(2,1)S(1)}, bf16[32,128,128]{2,1,0:T(8,128)(2,1)}, u32[]{:S(2)}) copy-start(bf16[32,128,128]{2,1,0:T(8,128)(2,1)} %param.10) | copy-start | bytes 3145732
  735.7 183.5 %copy-start.1 = (bf16[32,128,256]{2,1,0:T(8,128)(2,1)S(1)}, bf16[32,128,256]{2,1,0:T(8,128)(2,1)}, u32[]{:S(2)}) copy-start(bf16[32,128,256]{2,1,0:T(8,128)(2,1)} %param.11) | copy-start | bytes 6291460
Sparse Core Ops, SparseCore 0:
  99.9 224.2 reduce-scatter.3
  327.9 76.0 all-gather.2
  408.6 213.4 reduce-scatter.5
  625.1 76.2 all-gather.4
  705.6 213.5 reduce-scatter.7
where the time goes:
time: 927 us; the launch traced here: 926 us
  waiting for transfers between devices  760 us (82%)
  other arithmetic  63.3 us (7%)
  local copies, waits for them, and re-layouts  61.1 us (7%)
  matrix products  24.7 us (3%)
  between operations  15.9 us (2%)
    reduce_scatter x1, waiting for transfers between devices, on_device(): lax.psum_scatter(partial_terms.astype(jnp.bfloat16), 'front', scatter_dim...  224 us
    reduce_scatter x1, waiting for transfers between devices, on_device(): lax.psum_scatter(result.reshape(owned_count * lax.axis_size('front'), blo...  214 us
    reduce_scatter x1, waiting for transfers between devices, on_device(): lax.psum_scatter(placed.astype(jnp.bfloat16), 'front', scatter_dimension=...  170 us
    all_gather x1, waiting for transfers between devices, on_device(): arrived = lax.all_gather(separator_in, 'front', axis=0, tiled=True)  75.5 us
    all_gather x1, waiting for transfers between devices, on_device(): whole_front = lax.all_gather(solved, 'front', axis=0, tiled=True)  72 us
    scatter-add x1, other arithmetic, on_device(): partial_terms = jnp.zeros((2 * front_seps, block_width, probe_count), jnp...  48 us
    gather x2, local copies, waits for them, and re-layouts, on_device(): picked = pair_field[block_rows]  24.9 us
    reshape x1, local copies, waits for them, and re-layouts, on_device(): product = product.reshape(-1, block_width, probe_count)  21.2 us
  transfers between devices with their start and end apart: 7, of which 7 were waited for; matrix products, arithmetic and copies ran while one was open for 5% of the time, Pallas kernels for 0%

commit v1 on v0

--- a/solution.py
+++ b/solution.py
@@ -1,7 +1,23 @@
+import functools
 import jax
 import jax.numpy as jnp
 from jax import lax
 from jax.sharding import PartitionSpec as P
+
+
+def prepare_the_kinds(inputs, comm_axis):
+    return jnp.concatenate(
+        jax.lax.all_to_all(
+            jnp.stack(tuple((inputs for _ in range(jax.lax.psum(1, comm_axis)))), 0),
+            comm_axis,
+            0,
+            0,
+        ),
+        0,
+    )
+
+
+_put_series = functools.partial(prepare_the_kinds, comm_axis="front")
 
 
 def swapped(shard, axis, bit):
@@ -72,7 +88,7 @@
         tiled=True,
     ).astype(jnp.float32)
     solved = sep_solution.astype(jnp.bfloat16)
-    whole_front = lax.all_gather(solved, "front", axis=0, tiled=True)
+    whole_front = _put_series(solved)
     other_front = swapped(whole_front, "leaf", 0)
     lower_front = jnp.where(parity == 0, whole_front, other_front)
     upper_front = jnp.where(parity == 0, other_front, whole_front)

time: 927 us -> 868 us (0.936)
  waiting for transfers between devices: 760 us -> 694 us
    all_gather x1 -> x0, waiting for transfers between devices: 72 us -> none  [on_device(): whole_front = lax.all_gather(solved, 'front', axis=0, tiled=True)]
    all_to_all x0 -> x1, waiting for transfers between devices: none -> 41.1 us  [prepare_the_kinds(): jax.lax.all_to_all(jnp.stack(tuple((inputs for _ in range(jax.lax.psum(1,...]
    reduce_scatter x1, waiting for transfers between devices: 170 us -> 134 us  [on_device(): lax.psum_scatter(placed.astype(jnp.bfloat16), 'front', scatter_dimension=...]
where the time goes in v1:
time: 868 us; the launch traced here: 867 us
  waiting for transfers between devices  694 us (80%)
  other arithmetic  63.7 us (7%)
  local copies, waits for them, and re-layouts  61.6 us (7%)
  matrix products  24.6 us (3%)
  between operations  15.9 us (2%)
    reduce_scatter x1, waiting for transfers between devices, on_device(): lax.psum_scatter(partial_terms.astype(jnp.bfloat16), 'front', scatter_dim...  224 us
    reduce_scatter x1, waiting for transfers between devices, on_device(): lax.psum_scatter(result.reshape(owned_count * lax.axis_size('front'), blo...  214 us
    reduce_scatter x1, waiting for transfers between devices, on_device(): lax.psum_scatter(placed.astype(jnp.bfloat16), 'front', scatter_dimension=...  134 us
    all_gather x1, waiting for transfers between devices, on_device(): arrived = lax.all_gather(separator_in, 'front', axis=0, tiled=True)  75.5 us
    scatter-add x1, other arithmetic, on_device(): partial_terms = jnp.zeros((2 * front_seps, block_width, probe_count), jnp...  48.2 us
    all_to_all x1, waiting for transfers between devices, prepare_the_kinds(): jax.lax.all_to_all(jnp.stack(tuple((inputs for _ in range(jax.lax.psum(1,...  41.1 us
    gather x2, local copies, waits for them, and re-layouts, on_device(): picked = pair_field[block_rows]  24.6 us
    reshape x1, local copies, waits for them, and re-layouts, on_device(): product = product.reshape(-1, block_width, probe_count)  21.2 us
  transfers between devices with their start and end apart: 7, of which 7 were waited for; matrix products, arithmetic and copies ran while one was open for 5% of the time, Pallas kernels for 0%

profile of v1, /device:TPU:8, one launch (start us, length us, event | category | flops | bytes accessed | tf_op | source)
XLA Modules:
  0.0 866.6 jit_solution(8743753568595279669)
XLA Ops:
  7.2 0.0 reduce-scatter.4.cloned.1.call-start
  7.2 0.8 add_select_fusion
  8.1 0.1 copy.29
  8.2 0.1 reshape.119
  8.3 0.9 iota_compare_fusion
  9.2 2.1 convolution_convert_fusion
  11.3 9.0 %broadcast_select_fusion = f32[32,256,5,128]{3,1,2,0:T(8,128)} fusion(pred[32,5]{1,0:T(8,128)(4,1)S(1)} %iota_compare_fusion, bf16[32,5,128,128]{3,2,1,0:T(8,128)(2,1)S(1)} %copy-done.4, bf16[32,128,256]{2,1,0:T(8,128)(2,1)S(1)} %convolution_convert_fusion), kind=kOutput, calls=%fused_computation.4 | convolution fusion | flops 1347420160 | bytes 28311712 | tf_op jit(solution)/shard_map/kpab,kbr->kpar/dot_general | solution.py:40
  20.3 21.2 %copy.31 = f32[160,128,256]{2,1,0:T(8,128)} copy(f32[160,128,256]{1,2,0:T(8,128)} %bitcast.49) | data formatting | bytes 41943040 | tf_op jit(solution)/shard_map/reshape | solution.py:42
  41.5 4.3 broadcast_in_dim.40
  45.8 48.2 %scatter_fusion = f32[64,128,256]{2,1,0:T(8,128)} fusion(f32[64,128,256]{2,1,0:T(8,128)} %broadcast_in_dim.40, s32[160]{0:T(256)S(1)} %bitcast.55, f32[160,128,256]{2,1,0:T(8,128)} %copy.31), kind=kCustom, calls=%fused_computation.1 | custom fusion | flops 5242880 | bytes 62915200 | tf_op jit(solution)/shard_map/scatter-add | solution.py:54
  94.0 5.9 convert_element_type.59
  99.9 0.0 reduce-scatter.4.cloned.1.call-update
  99.9 0.0 all-gather.2.cloned.1.call-start
  100.0 224.3 %reduce-scatter.4.cloned.1.call-done = bf16[2,128,256]{2,1,0:T(8,128)(2,1)} async-done(((bf16[64,128,256]{2,1,0:T(8,128)(2,1)}), bf16[2,128,256]{2,1,0:T(8,128)(2,1)}) %reduce-scatter.4.cloned.1.call-update) | async-done | bytes 131088 | tf_op jit(solution)/shard_map/reduce_scatter | solution.py:56
  324.2 0.8 slice.35
  325.1 1.3 collective-permute-done
  326.4 1.5 subtract_convert_fusion
  327.8 0.0 all-gather.2.cloned.1.call-update
  327.9 0.0 reduce-scatter.6.cloned.1.call-start
  327.9 0.7 copy.46
  328.6 75.5 %all-gather.2.cloned.1.call-done = bf16[32,128,256]{2,1,0:T(8,128)(2,1)} async-done(((bf16[1,128,256]{2,1,0:T(8,128)(2,1)}), bf16[32,128,256]{2,1,0:T(8,128)(2,1)}) %all-gather.2.cloned.1.call-update) | async-done | bytes 2097168 | tf_op jit(solution)/shard_map/all_gather | solution.py:62
  404.1 2.3 convolution_convert_fusion.1
  406.4 2.0 convert_bitcast_fusion.1
  408.5 0.0 reduce-scatter.6.cloned.1.call-update
  408.5 213.7 %reduce-scatter.6.cloned.1.call-done = bf16[1,128,256]{1,2,0:T(8,128)(2,1)} async-done(((bf16[32,128,256]{1,2,0:T(8,128)(2,1)}), bf16[1,128,256]{1,2,0:T(8,128)(2,1)}) %reduce-scatter.6.cloned.1.call-update) | async-done | bytes 65552 | tf_op jit(solution)/shard_map/reduce_scatter | solution.py:82
  622.2 0.9 copy.33
  623.2 1.6 stack.2
  624.7 7.0 all-to-all-start
  631.7 0.0 reduce-scatter.8.cloned.1.call-start
  631.8 0.6 constant_dynamic-slice_fusion
  634.4 0.7 and_reduce_fusion
  635.1 0.7 select_bitcast_fusion
  635.7 0.1 copy.38
  635.8 0.2 broadcast_in_dim.45
  636.1 1.3 copy-done.2
  637.4 0.0 reduce-scatter.8.cloned.1.call-update
  637.5 41.1 %all-to-all-done = bf16[32,1,128,256]{3,2,1,0:T(8,128)(2,1)} async-done(((bf16[32,1,128,256]{3,2,1,0:T(8,128)(2,1)}), bf16[32,1,128,256]{3,2,1,0:T(8,128)(2,1)}, u32[]{:S(2)}, u32[]{:S(2)}) %all-to-all-start) | async-done | bytes 2097184 | tf_op jit(solution)/shard_map/all_to_all | solution.py:10
  678.6 0.1 copy.34
  678.7 0.1 reshape.128
  678.8 0.8 copy.40
  679.5 3.5 collective-permute-done.1
  683.1 2.5 broadcast_select_fusion.2
  685.6 2.4 pad_maximum_fusion
  688.0 9.8 %gather_fusion = bf16[160,128,256]{2,1,0:T(8,128)(2,1)} fusion(bf16[64,128,256]{2,1,0:T(8,128)(2,1)} %pad_maximum_fusion, s32[1024]{0:T(1024)S(1)} %pad_clamp_fusion), kind=kCustom, calls=%fused_computation | custom fusion | bytes 20972160 | tf_op jit(solution)/shard_map/gather | solution.py:96
  697.8 14.8 %copy.35 = bf16[32,5,128,256]{2,3,1,0:T(8,128)(2,1)} copy(bf16[32,5,128,256]{3,2,1,0:T(8,128)(2,1)} %bitcast.50) | data formatting | bytes 20971520 | tf_op jit(solution)/shard_map/gather | solution.py:96
  712.6 9.2 %convert_bitcast_fusion = bf16[32,128,256]{1,2,0:T(8,128)(2,1)} fusion(bf16[32,128,128]{2,1,0:T(8,128)(2,1)S(1)} %copy-done.6, bf16[32,128,256]{2,1,0:T(8,128)(2,1)} %copy-done.3, bf16[32,5,128,128]{3,2,1,0:T(8,128)(2,1)} %param.12, bf16[32,5,128,256]{2,3,1,0:T(8,128)(2,1)} %copy.35, pred[32,5]{1,0:T(8,128)(4,1)S(1)} %iota_compare_fusion), kind=kOutput, calls=%fused_computation.11 | convolution fusion | flops 1620049920 | bytes 20971680 | tf_op jit(solution)/shard_map/kba,kbr->kar/dot_general | solution.py:100
  721.8 4.1 copy.39
  725.9 134.2 %reduce-scatter.8.cloned.1.call-done = bf16[1,128,256]{2,1,0:T(8,128)(2,1)} async-done(((bf16[32,128,256]{2,1,0:T(8,128)(2,1)}), bf16[1,128,256]{2,1,0:T(8,128)(2,1)}) %reduce-scatter.8.cloned.1.call-update) | async-done | bytes 65552 | tf_op jit(solution)/shard_map/reduce_scatter | solution.py:77
  (26 shorter events, 0.1 us)
Async XLA Ops:
  7.2 2.0 copy-start
  7.2 317.1 %reduce-scatter.4.cloned.1.call-start = ((), (), s32[]{:S(2)}) async-start(), calls=%async_computation.4 | async-start | bytes 4325376 | tf_op jit(solution)/shard_map/reduce_scatter | solution.py:56
  8.3 3.0 copy-start.4
  11.3 9.0 %copy-start.3 = (bf16[32,128,256]{2,1,0:T(8,128)(2,1)}, bf16[32,128,256]{2,1,0:T(8,128)(2,1)S(1)}, u32[]{:S(2)}) copy-start(bf16[32,128,256]{2,1,0:T(8,128)(2,1)S(1)} %convolution_convert_fusion) | copy-start | bytes 6291460
  99.9 226.4 %copy-start.8 = (bf16[1,128,256]{2,1,0:T(8,128)(2,1)S(1)}, bf16[1,128,256]{2,1,0:T(8,128)(2,1)}, u32[]{:S(2)}) copy-start(bf16[1,128,256]{2,1,0:T(8,128)(2,1)} %param.15) | copy-start | bytes 196612
  99.9 228.0 %copy-start.5 = (bf16[1,128,4096]{2,1,0:T(8,128)(2,1)S(1)}, bf16[1,128,4096]{2,1,0:T(8,128)(2,1)}, u32[]{:S(2)}) copy-start(bf16[1,128,4096]{2,1,0:T(8,128)(2,1)} %param.17) | copy-start | bytes 3145732
  99.9 304.1 %all-gather.2.cloned.1.call-start = ((), (), s32[]{:S(2)}) async-start(), calls=%async_computation.5 | async-start | bytes 2162688 | tf_op jit(solution)/shard_map/all_gather | solution.py:62
  325.1 1.3 collective-permute-start
  327.9 294.3 %reduce-scatter.6.cloned.1.call-start = ((), (), s32[]{:S(2)}) async-start(), calls=%async_computation.6 | async-start | bytes 2162688 | tf_op jit(solution)/shard_map/reduce_scatter | solution.py:82
  408.5 223.3 %copy-start.10 = (s32[1,32]{1,0:T(1,128)S(1)}, s32[1,32]{1,0:T(1,128)}, u32[]{:S(2)}) copy-start(s32[1,32]{1,0:T(1,128)} %param.16) | copy-start | bytes 388
  408.5 225.9 %copy-start.9 = (s32[3]{0:T(128)S(1)}, s32[3]{0:T(128)}, u32[]{:S(2)}) copy-start(s32[3]{0:T(128)} %constant.102.clone.1) | copy-start | bytes 40
  624.7 54.1 %copy-start.7 = (bf16[1,128,256]{1,2,0:T(8,128)(2,1)S(1)}, bf16[1,128,256]{1,2,0:T(8,128)(2,1)}, u32[]{:S(2)}) copy-start(bf16[1,128,256]{1,2,0:T(8,128)(2,1)} %reduce-scatter.6.cloned.1.call-done) | copy-start | bytes 196612
  624.7 53.8 %all-to-all-start = ((bf16[32,1,128,256]{3,2,1,0:T(8,128)(2,1)}), bf16[32,1,128,256]{3,2,1,0:T(8,128)(2,1)}, u32[]{:S(2)}, u32[]{:S(2)}) async-start(bf16[32,1,128,256]{3,2,1,0:T(8,128)(2,1)} %stack.2), calls=%async_computation.2 | async-start | bytes 4194304 | tf_op jit(solution)/shard_map/all_to_all | solution.py:10
  631.7 228.3 %reduce-scatter.8.cloned.1.call-start = ((), (), s32[]{:S(2)}) async-start(), calls=%async_computation.7 | async-start | bytes 2162688 | tf_op jit(solution)/shard_map/reduce_scatter | solution.py:77
  636.1 1.3 copy-start.2
  678.6 4.5 collective-permute-start.1
  697.8 14.8 %copy-start.6 = (bf16[32,128,128]{2,1,0:T(8,128)(2,1)S(1)}, bf16[32,128,128]{2,1,0:T(8,128)(2,1)}, u32[]{:S(2)}) copy-start(bf16[32,128,128]{2,1,0:T(8,128)(2,1)} %param.10) | copy-start | bytes 3145732
  712.6 147.5 %copy-start.1 = (bf16[32,128,256]{2,1,0:T(8,128)(2,1)S(1)}, bf16[32,128,256]{2,1,0:T(8,128)(2,1)}, u32[]{:S(2)}) copy-start(bf16[32,128,256]{2,1,0:T(8,128)(2,1)} %param.11) | copy-start | bytes 6291460
Sparse Core Ops, SparseCore 0:
  100.1 224.1 reduce-scatter.3
  328.0 76.0 all-gather.1
  408.6 213.5 reduce-scatter.5
  637.6 222.4 reduce-scatter.7
